TPU v7x, 256 devices: a whole 4x4x8 slice. The times are simulated.
256 devices in a mesh: sy: 16 (over z_lo, y, core), sx: 4 (over x), cls: 4 (over z_hi).
Axes of the slice: x: 4, y: 4, z: 8 (z_hi: 4, z_lo: 2; z = z_hi * 2 + z_lo), core: 2. Of those that a mesh axis runs over, the one named last changes fastest.
Arguments:
- adjoint_final: float32 [64, 1024, 1536], P('cls', 'sy', 'sx'), may hold values from -6 to 6
- stored_states: bfloat16 [2, 64, 1024, 1536], P(None, 'cls', 'sy', 'sx'), may hold values from 0.049804688 to 2
- habitat: int32 [1024, 1536], P('sy', 'sx'), may hold values from 0 to 7
- growth: float32 [64, 64], replicated, may hold values from -0.75 to 0.75
- survival: float32 [8, 64], replicated, may hold values from 0.3 to 1
- fecundity: float32 [8, 64], replicated, may hold values from 0.1 to 3
- recruit: float32 [64], replicated, may hold values from 0 to 0.25
- disp_rows: float32 [15], replicated, may hold values from 0.02 to 0.2
- disp_cols: float32 [15], replicated, may hold values from 0.02 to 0.2
Outputs:
- adjoint_start: float32 [64, 1024, 1536], P('cls', 'sy', 'sx')
- survival_sens: float32 [2, 64, 1024, 1536], P(None, 'cls', 'sy', 'sx')
All inputs are finite; a program needn't handle non-finite values.
Results may differ from a plain program's by a relative error of at most 0.0003.
Values sent between devices are 32-bit elements; how exact they have to be, the bound alone decides.
A program may use at most 64 MiB of HBM per device.

v0:
```python
import jax
import jax.numpy as jnp
from jax import lax
from jax.sharding import PartitionSpec as P


def with_halo(value, sides, width):
    for axis, dim in sides:
        count, length = (lax.axis_size(axis), value.shape[dim])
        up = [(i, (i + 1) % count) for i in range(count - 1)]
        down = [(j, i) for i, j in up]
        last = lax.slice_in_dim(value, length - width, length, axis=dim)
        leading = lax.slice_in_dim(value, 0, width, axis=dim)
        before = lax.ppermute(last, axis, up)
        after = lax.ppermute(leading, axis, down)
        value = jnp.concatenate([before, value, after], axis=dim)
    return value


def pass_rows(padded, weights, length):
    result = weights[0] * padded[0:length, :]
    for offset in range(1, weights.shape[0]):
        result = result + weights[offset] * padded[offset : offset + length, :]
    return result


def pass_cols(padded, weights, length):
    result = weights[0] * padded[:, 0:length]
    for offset in range(1, weights.shape[0]):
        result = result + weights[offset] * padded[:, offset : offset + length]
    return result


def per_device(
    adjoint_final,
    stored_states,
    habitat,
    growth,
    survival,
    fecundity,
    recruit,
    disp_rows,
    disp_cols,
):
    local_count = adjoint_final.shape[0]
    grid_rows = adjoint_final.shape[1]
    grid_cols = adjoint_final.shape[2]
    reach_cells = disp_rows.shape[0] // 2
    first_class = lax.axis_index("cls") * local_count
    levels = jnp.arange(survival.shape[0], dtype=jnp.int32)
    sensitivity = [None] * stored_states.shape[0]
    indicator = (habitat[None, :, :] == levels[:, None, None]).astype(jnp.float32)
    tables = lax.dynamic_slice_in_dim(jnp.stack([survival, fecundity]), first_class, local_count, 2)
    cell_rates = jnp.einsum("thj,hyx->tjyx", tables, indicator, precision=lax.Precision.HIGHEST)
    growth_rows = lax.dynamic_slice_in_dim(growth, first_class, local_count, 0)
    recruit_local = lax.dynamic_slice_in_dim(recruit, first_class, local_count, 0)
    adjoint = adjoint_final
    for period in range(stored_states.shape[0] - 1, -1, -1):
        current = adjoint
        carried = lax.psum_scatter(
            jnp.einsum("ij,iyx->jyx", growth_rows, current, precision=lax.Precision.HIGHEST),
            "cls",
            scatter_dimension=0,
            tiled=True,
        )
        seed_local = jnp.einsum(
            "i,iyx->yx", recruit_local, current, precision=lax.Precision.HIGHEST
        )
        seed_value = lax.psum(seed_local, "cls")
        padded = with_halo(seed_value, (("sy", 0), ("sx", 1)), reach_cells)
        across = pass_rows(padded, disp_rows, grid_rows)
        spread = pass_cols(across, disp_cols, grid_cols)
        sensitivity[period] = stored_states[period].astype(jnp.float32) * carried
        adjoint = cell_rates[0] * carried + cell_rates[1] * spread[None]
    return (adjoint, jnp.stack(sensitivity))


def solution(mesh):
    placed = (
        P("cls", "sy", "sx"),
        P(None, "cls", "sy", "sx"),
        P("sy", "sx"),
        P(),
        P(),
        P(),
        P(),
        P(),
        P(),
    )
    return jax.shard_map(
        per_device,
        mesh=mesh,
        in_specs=placed,
        out_specs=(P("cls", "sy", "sx"), P(None, "cls", "sy", "sx")),
        check_vma=False,
    )
```

profile of v0, /device:TPU:32, one launch (start us, length us, event | category | flops | bytes accessed | tf_op | source)
XLA Modules:
  0.0 370.0 jit_solution(17312446841709403750)
XLA Ops:
  7.2 0.0 all-reduce.3.cloned.1.call-start
  7.2 1.3 copy-done
  8.6 2.4 fusion.2
  11.0 0.6 copy.34
  11.6 0.0 reduce-scatter.3.cloned.1.call-start
  11.7 7.3 %fusion.4 = f32[64,64,384]{2,0,1:T(8,128)} fusion(f32[16,64,384]{2,1,0:T(8,128)S(1)} %copy-done, f32[64,64]{1,0:T(8,128)S(1)} %copy-done.7, s32[]{:T(128)S(6)} %select_n.2), kind=kOutput, calls=%fused_computation.11 | convolution fusion | flops 301989888 | bytes 7872516 | tf_op jit(solution)/shard_map/ij,iyx->jyx/dot_general | solution.py:61
  19.0 0.0 all-reduce.5.cloned.1.call-start
  19.1 1.3 copy-done.3
  20.4 1.4 fusion.85
  21.8 3.2 fusion.7
  25.0 38.1 %all-reduce.3.cloned.1.call-done = f32[64,384]{1,0:T(8,128)} async-done(((f32[64,384]{1,0:T(8,128)}), f32[64,384]{1,0:T(8,128)}) %all-reduce.3.cloned.1.call-update) | async-done | bytes 98320 | tf_op jit(solution)/shard_map/psum | solution.py:69
  63.1 0.7 fusion.87
  63.8 1.9 collective-permute-start
  65.7 5.8 %collective-permute-start.1 = (f32[7,384]{1,0:T(8,128)S(1)}, f32[7,384]{1,0:T(8,128)S(1)}, u32[]{:S(2)}, u32[]{:S(2)}) collective-permute-start(f32[7,384]{1,0:T(8,128)S(1)} %get-tuple-element.17), channel_id=1, source_target_pairs={{16,0},{32,16},{48,32},{64,48},{80,64},{96,80},{112,96},{128,112},... | collective-permute-start | bytes 32264 | tf_op jit(solution)/shard_map/ppermute | solution.py:15
  71.5 0.7 fusion.89
  72.2 0.7 collective-permute-done.1
  72.9 0.9 pad_maximum_fusion.8
  73.7 3.4 collective-permute-start.2
  77.1 1.3 collective-permute-start.3
  78.4 0.7 fusion.88
  79.1 3.9 %collective-permute-done.3 = f32[78,7]{1,0:T(8,128)S(1)} collective-permute-done((f32[78,7]{1,0:T(8,128)S(1)}, f32[78,7]{1,0:T(8,128)S(1)}, u32[]{:S(2)}, u32[]{:S(2)}) %collective-permute-start.3) | collective-permute-done | bytes 2216 | tf_op jit(solution)/shard_map/ppermute | solution.py:15
  83.0 1.0 pad_maximum_fusion.1
  84.0 9.5 %fusion.24 = f32[64,398]{1,0:T(8,128)S(1)} fusion(f32[78,398]{1,0:T(8,128)S(1)} %pad_maximum_fusion.1, f32[]{:T(128)} %bitcast.25, f32[]{:T(128)} %bitcast.24, f32[]{:T(128)} %bitcast.23, f32[]{:T(128)} %bitcast.22, f32[]{:T(128)} %bitcast.21, f32[]{:T(128)} %bitcast.20, f32[]{:T(128)} %bitcast.19, f32[]{:T(128)} %bitcast.18, f32[]{:T(128)} %bitcast.17, ...), kind=kLoop, calls=%fused_computation.51 | loop fusion | flops 738688 | bytes 1630268 | tf_op jit(solution)/shard_map/add | solution.py:23
  93.5 9.7 %fusion.52 = f32[64,384]{1,0:T(8,128)S(1)} fusion(f32[64,398]{1,0:T(8,128)S(1)} %fusion.24, f32[]{:T(128)} %bitcast.39, f32[]{:T(128)} %bitcast.38, f32[]{:T(128)} %bitcast.37, f32[]{:T(128)} %bitcast.36, f32[]{:T(128)} %bitcast.35, f32[]{:T(128)} %bitcast.34, f32[]{:T(128)} %bitcast.33, f32[]{:T(128)} %bitcast.32, f32[]{:T(128)} %bitcast.31, f32[]{:T(128)} %bitcast.30, ...), kind=kLoop, calls=%fused_computation.109 | loop fusion | flops 712704 | bytes 1572924 | tf_op jit(solution)/shard_map/add | solution.py:30
  103.2 79.4 %reduce-scatter.3.cloned.1.call-done = f32[16,64,384]{2,0,1:T(8,128)} async-done(((f32[64,64,384]{2,0,1:T(8,128)}), f32[16,64,384]{2,0,1:T(8,128)}) %reduce-scatter.3.cloned.1.call-update) | async-done | bytes 1572880 | tf_op jit(solution)/shard_map/reduce_scatter | solution.py:60
  182.6 4.5 %fusion = (f32[1,16,64,384]{3,1,2,0:T(8,128)}, f32[16,64,384]{2,0,1:T(8,128)S(1)}) fusion(f32[16,64,384]{2,0,1:T(8,128)} %reduce-scatter.3.cloned.1.call-done, bf16[1,16,64,384]{3,2,1,0:T(8,128)(2,1)} %get-tuple-element.7, f32[64,384]{1,0:T(8,128)S(1)} %fusion.52, f32[2,16,64,384]{3,1,2,0:T(8,128)} %fusion.7), kind=kLoop, calls=%fused_computation.4 | loop fusion | flops 1966080 | bytes 8749056 | tf_op jit(solution)/shard_map/stack | solution.py:75
  187.1 0.9 fusion.79
  188.0 0.7 copy.33
  188.6 0.0 reduce-scatter.5.cloned.1.call-start
  188.7 7.0 %fusion.71 = f32[64,64,384]{2,0,1:T(8,128)} fusion(f32[16,64,384]{2,0,1:T(8,128)S(1)} %get-tuple-element.9, f32[64,64]{1,0:T(8,128)S(1)} %copy-done.7, s32[]{:T(128)S(6)} %select_n.2), kind=kOutput, calls=%fused_computation.150 | convolution fusion | flops 301989888 | bytes 7872516 | tf_op jit(solution)/shard_map/ij,iyx->jyx/dot_general | solution.py:61
  195.7 41.6 %all-reduce.5.cloned.1.call-done = f32[64,384]{1,0:T(8,128)} async-done(((f32[64,384]{1,0:T(8,128)}), f32[64,384]{1,0:T(8,128)}) %all-reduce.5.cloned.1.call-update) | async-done | bytes 98320 | tf_op jit(solution)/shard_map/psum | solution.py:69
  237.3 0.7 fusion.86
  238.0 1.9 collective-permute-start.4
  240.0 5.9 %collective-permute-start.5 = (f32[7,384]{1,0:T(8,128)S(1)}, f32[7,384]{1,0:T(8,128)S(1)}, u32[]{:S(2)}, u32[]{:S(2)}) collective-permute-start(f32[7,384]{1,0:T(8,128)S(1)} %get-tuple-element.15), channel_id=1, source_target_pairs={{16,0},{32,16},{48,32},{64,48},{80,64},{96,80},{112,96},{128,112},... | collective-permute-start | bytes 32264 | tf_op jit(solution)/shard_map/ppermute | solution.py:15
  245.9 1.2 collective-permute-done.5
  247.1 0.9 pad_maximum_fusion.5
  247.9 3.4 collective-permute-start.6
  251.3 1.3 collective-permute-start.7
  252.6 0.4 collective-permute-done.6
  253.0 4.2 %collective-permute-done.7 = f32[78,7]{1,0:T(8,128)S(1)} collective-permute-done((f32[78,7]{1,0:T(8,128)S(1)}, f32[78,7]{1,0:T(8,128)S(1)}, u32[]{:S(2)}, u32[]{:S(2)}) %collective-permute-start.7) | collective-permute-done | bytes 2216 | tf_op jit(solution)/shard_map/ppermute | solution.py:15
  257.2 1.0 pad_maximum_fusion.2
  258.3 9.6 %fusion.10 = f32[64,398]{1,0:T(8,128)S(1)} fusion(f32[78,398]{1,0:T(8,128)S(1)} %pad_maximum_fusion.2, f32[]{:T(128)} %bitcast.25, f32[]{:T(128)} %bitcast.24, f32[]{:T(128)} %bitcast.23, f32[]{:T(128)} %bitcast.22, f32[]{:T(128)} %bitcast.21, f32[]{:T(128)} %bitcast.20, f32[]{:T(128)} %bitcast.19, f32[]{:T(128)} %bitcast.18, f32[]{:T(128)} %bitcast.17, ...), kind=kLoop, calls=%fused_computation.22 | loop fusion | flops 738688 | bytes 1630268 | tf_op jit(solution)/shard_map/add | solution.py:23
  267.8 9.7 %fusion.38 = f32[64,384]{1,0:T(8,128)S(1)} fusion(f32[64,398]{1,0:T(8,128)S(1)} %fusion.10, f32[]{:T(128)} %bitcast.39, f32[]{:T(128)} %bitcast.38, f32[]{:T(128)} %bitcast.37, f32[]{:T(128)} %bitcast.36, f32[]{:T(128)} %bitcast.35, f32[]{:T(128)} %bitcast.34, f32[]{:T(128)} %bitcast.33, f32[]{:T(128)} %bitcast.32, f32[]{:T(128)} %bitcast.31, f32[]{:T(128)} %bitcast.30, ...), kind=kLoop, calls=%fused_computation.80 | loop fusion | flops 712704 | bytes 1572924 | tf_op jit(solution)/shard_map/add | solution.py:30
  277.5 78.3 %reduce-scatter.5.cloned.1.call-done = f32[16,64,384]{2,0,1:T(8,128)} async-done(((f32[64,64,384]{2,0,1:T(8,128)}), f32[16,64,384]{2,0,1:T(8,128)}) %reduce-scatter.5.cloned.1.call-update) | async-done | bytes 1572880 | tf_op jit(solution)/shard_map/reduce_scatter | solution.py:60
  355.9 3.2 fusion.1
  359.0 0.2 pad_maximum_fusion
  359.3 2.6 copy.15
  361.9 1.6 copy.14
  (27 shorter events, 0.1 us)
Async XLA Ops:
  7.2 1.4 copy-start
  7.2 4.5 %copy-start.7 = (f32[64,64]{1,0:T(8,128)S(1)}, f32[64,64]{1,0:T(8,128)}, u32[]{:S(2)}) copy-start(f32[64,64]{1,0:T(8,128)} %param.12) | copy-start | bytes 49156
  7.2 55.9 %all-reduce.3.cloned.1.call-start = ((), (), s32[]{:S(2)}) async-start(), calls=%async_computation.3 | async-start | bytes 196608 | tf_op jit(solution)/shard_map/psum | solution.py:69
  11.6 171.0 %reduce-scatter.3.cloned.1.call-start = ((), (), s32[]{:S(2)}) async-start(), calls=%async_computation.2 | async-start | bytes 7864320 | tf_op jit(solution)/shard_map/reduce_scatter | solution.py:60
  18.9 1.4 copy-start.3
  19.0 2.8 copy-start.6
  19.0 2.8 copy-start.8
  19.0 2.8 copy-start.9
  19.0 218.3 %all-reduce.5.cloned.1.call-start = ((), (), s32[]{:S(2)}) async-start(), calls=%async_computation.5 | async-start | bytes 196608 | tf_op jit(solution)/shard_map/psum | solution.py:69
  21.8 49.7 %copy-start.4 = (f32[15]{0:T(128)S(1)}, f32[15]{0:T(128)}, u32[]{:S(2)}) copy-start(f32[15]{0:T(128)} %param.16) | copy-start | bytes 184
  21.8 56.6 %copy-start.5 = (f32[15]{0:T(128)S(1)}, f32[15]{0:T(128)}, u32[]{:S(2)}) copy-start(f32[15]{0:T(128)} %param.17) | copy-start | bytes 184
  63.8 8.4 %collective-permute-start = (f32[7,384]{1,0:T(8,128)S(1)}, f32[7,384]{1,0:T(8,128)S(1)}, u32[]{:S(2)}, u32[]{:S(2)}) collective-permute-start(f32[7,384]{1,0:T(8,128)S(1)} %get-tuple-element.16), channel_id=1, source_target_pairs={{0,16},{16,32},{32,48},{48,64},{64,80},{80,96},{96,112},{112,128},... | collective-permute-start | bytes 32264 | tf_op jit(solution)/shard_map/ppermute | solution.py:14
  65.7 7.1 %collective-permute-start.1 = (f32[7,384]{1,0:T(8,128)S(1)}, f32[7,384]{1,0:T(8,128)S(1)}, u32[]{:S(2)}, u32[]{:S(2)}) collective-permute-start(f32[7,384]{1,0:T(8,128)S(1)} %get-tuple-element.17), channel_id=1, source_target_pairs={{16,0},{32,16},{48,32},{64,48},{80,64},{96,80},{112,96},{128,112},... | collective-permute-start | bytes 32264 | tf_op jit(solution)/shard_map/ppermute | solution.py:15
  73.7 5.4 %collective-permute-start.2 = (f32[78,7]{1,0:T(8,128)S(1)}, f32[78,7]{1,0:T(8,128)S(1)}, u32[]{:S(2)}, u32[]{:S(2)}) collective-permute-start(f32[78,7]{1,0:T(8,128)S(1)} %get-tuple-element.12), channel_id=1, source_target_pairs={{0,4},{4,8},{8,12},{1,5},{5,9},{9,13},{2,6},{6,10},{10,14},{3,7},{... | collective-permute-start | bytes 6560 | tf_op jit(solution)/shard_map/ppermute | solution.py:14
  77.1 5.9 %collective-permute-start.3 = (f32[78,7]{1,0:T(8,128)S(1)}, f32[78,7]{1,0:T(8,128)S(1)}, u32[]{:S(2)}, u32[]{:S(2)}) collective-permute-start(f32[78,7]{1,0:T(8,128)S(1)} %get-tuple-element.13), channel_id=1, source_target_pairs={{4,0},{8,4},{12,8},{5,1},{9,5},{13,9},{6,2},{10,6},{14,10},{7,3},{... | collective-permute-start | bytes 6560 | tf_op jit(solution)/shard_map/ppermute | solution.py:15
  182.6 4.5 %copy-start.10 = (f32[64]{0:T(128)S(1)}, f32[64]{0:T(128)}, u32[]{:S(2)}) copy-start(f32[64]{0:T(128)} %param.15) | copy-start | bytes 772
  188.6 167.2 %reduce-scatter.5.cloned.1.call-start = ((), (), s32[]{:S(2)}) async-start(), calls=%async_computation.4 | async-start | bytes 7864320 | tf_op jit(solution)/shard_map/reduce_scatter | solution.py:60
  238.0 7.9 %collective-permute-start.4 = (f32[7,384]{1,0:T(8,128)S(1)}, f32[7,384]{1,0:T(8,128)S(1)}, u32[]{:S(2)}, u32[]{:S(2)}) collective-permute-start(f32[7,384]{1,0:T(8,128)S(1)} %get-tuple-element.14), channel_id=1, source_target_pairs={{0,16},{16,32},{32,48},{48,64},{64,80},{80,96},{96,112},{112,128},... | collective-permute-start | bytes 32264 | tf_op jit(solution)/shard_map/ppermute | solution.py:14
  240.0 7.1 %collective-permute-start.5 = (f32[7,384]{1,0:T(8,128)S(1)}, f32[7,384]{1,0:T(8,128)S(1)}, u32[]{:S(2)}, u32[]{:S(2)}) collective-permute-start(f32[7,384]{1,0:T(8,128)S(1)} %get-tuple-element.15), channel_id=1, source_target_pairs={{16,0},{32,16},{48,32},{64,48},{80,64},{96,80},{112,96},{128,112},... | collective-permute-start | bytes 32264 | tf_op jit(solution)/shard_map/ppermute | solution.py:15
  247.9 5.0 %collective-permute-start.6 = (f32[78,7]{1,0:T(8,128)S(1)}, f32[78,7]{1,0:T(8,128)S(1)}, u32[]{:S(2)}, u32[]{:S(2)}) collective-permute-start(f32[78,7]{1,0:T(8,128)S(1)} %get-tuple-element.10), channel_id=1, source_target_pairs={{0,4},{4,8},{8,12},{1,5},{5,9},{9,13},{2,6},{6,10},{10,14},{3,7},{... | collective-permute-start | bytes 6560 | tf_op jit(solution)/shard_map/ppermute | solution.py:14
  251.3 5.9 %collective-permute-start.7 = (f32[78,7]{1,0:T(8,128)S(1)}, f32[78,7]{1,0:T(8,128)S(1)}, u32[]{:S(2)}, u32[]{:S(2)}) collective-permute-start(f32[78,7]{1,0:T(8,128)S(1)} %get-tuple-element.11), channel_id=1, source_target_pairs={{4,0},{8,4},{12,8},{5,1},{9,5},{13,9},{6,2},{10,6},{14,10},{7,3},{... | collective-permute-start | bytes 6560 | tf_op jit(solution)/shard_map/ppermute | solution.py:15
  258.2 97.6 %copy-start.2 = (bf16[1,16,64,384]{3,2,1,0:T(8,128)(2,1)S(1)}, bf16[1,16,64,384]{3,2,1,0:T(8,128)(2,1)}, u32[]{:S(2)}) copy-start(bf16[1,16,64,384]{3,2,1,0:T(8,128)(2,1)} %get-tuple-element.6) | copy-start | bytes 2359300
  355.8 3.2 copy-start.1
Sparse Core Ops, SparseCore 0:
  11.7 51.2 all-reduce.2
  65.8 116.7 reduce-scatter.2
  188.8 48.4 all-reduce.4
  239.7 116.0 reduce-scatter.4
where the time goes:
time: 375 us; the launch traced here: 370 us
  waiting for transfers between devices  248 us (66%)
  other arithmetic  50 us (13%)
  starting transfers between devices  25 us (7%)
  matrix products  20.7 us (6%)
  between operations  14 us (4%)
  local copies, waits for them, and re-layouts  12.5 us (3%)
    reduce_scatter x2, waiting for transfers between devices, per_device(): lax.psum_scatter(jnp.einsum('ij,iyx->jyx', growth_rows, current, precisio...  158 us
    psum x2, waiting for transfers between devices, per_device(): seed_value = lax.psum(seed_local, 'cls')  79.7 us
    add x2, other arithmetic, pass_cols(): result = result + weights[offset] * padded[:, offset:offset + length]  19.4 us
    add x2, other arithmetic, pass_rows(): result = result + weights[offset] * padded[offset:offset + length, :]  19.1 us
    ppermute x4, starting transfers between devices, with_halo(): after = lax.ppermute(leading, axis, down)  14.3 us
    dot_general x2, matrix products, per_device(): jnp.einsum('ij,iyx->jyx', growth_rows, current, precision=lax.Precision.H...  14.3 us
    ppermute x4, starting transfers between devices, with_halo(): before = lax.ppermute(last, axis, up)  10.6 us
    ppermute x4, waiting for transfers between devices, with_halo(): after = lax.ppermute(leading, axis, down)  9.95 us
  transfers between devices with their start and end apart: 12, of which 9 were waited for; matrix products, arithmetic and copies ran while one was open for 17% of the time, Pallas kernels for 0%

commit v1 on v0

v1 whole, which is shorter than its diff:
```python
import functools

import jax
import jax.numpy as jnp
from jax import lax
from jax.experimental import pallas as pl
from jax.experimental.pallas import tpu as pltpu
from jax.sharding import PartitionSpec as P

MESH = pl.DeviceIdType.MESH
F32 = jnp.float32
BF16 = jnp.bfloat16
HIGH = lax.Precision.HIGHEST

SUB = 8
NEXT, OWN, REC, PREV, FAR = 0, 128, 256, 272, 400
ROWS_W = 528
HALO = 16
SIDE = 128


def dot_t(a, b):
    return lax.dot_general(a, b, (((1,), (1,)), ((), ())), precision=HIGH, preferred_element_type=F32)


def dot_h(a, b):
    return jnp.dot(a, b, precision=HIGH, preferred_element_type=F32)


def iota(shape, dim):
    return lax.broadcasted_iota(jnp.int32, shape, dim)


def split(x):
    hi = x.astype(BF16)
    return hi, (x - hi.astype(F32)).astype(BF16)


def kernel(
    a_hbm, st_hbm, hab, growth, surv, fec, rec, wr, wc,
    adj_out, sens_out,
    own, st_raw, st, gath, wh, wl, xh, xl, rs_all, tabs, c1_all, d_all, c1_snd, d_snd, planes, mid, seed0, sp1, sp0,
    lsem, send, recv,
):
    ncls = 4
    p = lax.axis_index("cls")
    sy, sx = lax.axis_index("sy"), lax.axis_index("sx")
    nsy, nsx = lax.axis_size("sy"), lax.axis_size("sx")
    right, left = lax.rem(p + 1, ncls), lax.rem(p + ncls - 1, ncls)
    below, above = lax.rem(sy + 1, nsy), lax.rem(sy + nsy - 1, nsy)
    east, west = lax.rem(sx + 1, nsx), lax.rem(sx + nsx - 1, nsx)
    classes, rows, cols = own.shape
    quarter = rows // ncls
    inner = pl.ds(SIDE, cols)

    load_a = pltpu.make_async_copy(a_hbm, own, lsem.at[0])
    load_s = pltpu.make_async_copy(st_hbm, st_raw, lsem.at[1])
    load_a.start()
    load_s.start()

    barrier = pltpu.get_barrier_semaphore()
    for where in ({"cls": left}, {"cls": right}, {"sy": above}, {"sy": below}, {"sx": west}, {"sx": east}):
        pl.semaphore_signal(barrier, inc=1, device_id=where, device_id_type=MESH)

    def q_row(ahead, s):
        return pl.multiple_of(lax.rem(p + ahead, ncls) * quarter + s * SUB, SUB)

    def remote(src, dst, k, where):
        return pltpu.make_async_remote_copy(
            src_ref=src, dst_ref=dst, send_sem=send.at[k], recv_sem=recv.at[k], device_id=where, device_id_type=MESH
        )

    to_right, to_left = {"cls": right}, {"cls": left}
    piece = lambda ref, row: ref.at[:, pl.ds(row, SUB), :]
    far_r = [remote(piece(own, q_row(1, s)), gath.at[0, s, 1], 0 + s, to_right) for s in range(2)]
    far_l = [remote(piece(own, q_row(2, s)), gath.at[1, s, 0], 2 + s, to_left) for s in range(2)]
    near_r = [remote(piece(own, q_row(0, s)), gath.at[1, s, 1], 4 + s, to_right) for s in range(2)]
    near_l = [remote(piece(own, q_row(3, s)), gath.at[0, s, 0], 6 + s, to_left) for s in range(2)]
    fwd_r = [remote(gath.at[0, s, 1], gath.at[1, s, 2], 8 + s, to_right) for s in range(2)]
    fwd_l = [remote(gath.at[1, s, 0], gath.at[0, s, 2], 10 + s, to_left) for s in range(2)]
    ret_c = [
        [remote(c1_snd.at[0, s], piece(c1_all, q_row(0, s)), 12 + s, to_left) for s in range(2)],
        [remote(c1_snd.at[1, s], piece(c1_all, q_row(3, s)), 14 + s, to_right) for s in range(2)],
    ]
    ret_d = [
        [remote(d_snd.at[0, s], piece(d_all, q_row(0, s)), 16 + s, to_left) for s in range(2)],
        [remote(d_snd.at[1, s], piece(d_all, q_row(3, s)), 18 + s, to_right) for s in range(2)],
    ]

    def seed_part(ahead):
        return planes.at[pl.ds(0, 2), pl.ds(pl.multiple_of(HALO + q_row(ahead, 0), SUB), quarter), inner]

    seed_l = remote(seed_part(0), seed_part(0), 20, to_left)
    seed_r = remote(seed_part(3), seed_part(3), 21, to_right)
    halo_d = remote(
        planes.at[:, pl.ds(rows, HALO), inner], planes.at[:, pl.ds(0, HALO), inner], 22, {"sy": below}
    )
    halo_u = remote(
        planes.at[:, pl.ds(HALO, HALO), inner], planes.at[:, pl.ds(HALO + rows, HALO), inner], 23, {"sy": above}
    )
    halo_e = remote(planes.at[:, :, pl.ds(cols, SIDE)], planes.at[:, :, pl.ds(0, SIDE)], 24, {"sx": east})
    halo_w = remote(
        planes.at[:, :, pl.ds(SIDE, SIDE)], planes.at[:, :, pl.ds(SIDE + cols, SIDE)], 25, {"sx": west}
    )

    pl.semaphore_wait(barrier, 6)
    load_a.wait()
    for s in range(2):
        far_r[s].start()
        far_l[s].start()
    for s in range(2):
        near_r[s].start()
        near_l[s].start()

    def place_of(rel):
        return ((p + rel) & (ncls - 1)) * classes

    r = iota((ROWS_W, 64), 0)
    base = jnp.where(r < OWN, place_of(1), jnp.where(r < REC, place_of(0), jnp.where(r < FAR, place_of(3), place_of(2))))
    off = jnp.where(r < REC, r & 127, (r - PREV) & 127) >> 3
    is_rec = (r >= REC) & (r < PREV)
    pick = jnp.where((base + off == iota((ROWS_W, 64), 1)) & ~is_rec, 1.0, 0.0).astype(F32)
    g = growth[...]
    by_source = dot_t(pick, g) + jnp.where(is_rec, rec[...], 0.0)
    c = iota((512, 64), 0)
    place_c = jnp.where(c < 128, place_of(1), jnp.where(c < 256, place_of(0), jnp.where(c < 384, place_of(3), place_of(2))))
    pick_c = jnp.where(place_c + ((c & 127) >> 3) == iota((512, 64), 1), 1.0, 0.0).astype(F32)
    full = dot_t(by_source, pick_c)
    full = jnp.where((iota(full.shape, 0) & 7) == (iota(full.shape, 1) & 7), full, 0.0)
    w_hi, w_lo = split(full)
    wh[...] = w_hi
    wl[...] = w_lo

    level = jnp.where((iota((64, 8), 0) >> 3) == iota((64, 8), 1), 1.0, 0.0).astype(F32)

    def expand(table):
        wide = dot_t(table, level)
        return jnp.where((iota(wide.shape, 0) & 7) == (iota(wide.shape, 1) & 7), wide, 0.0)

    s_tab, f_tab = surv[...], fec[...]
    pick_own = pick[OWN:REC]
    k_surv = expand(dot_t(pick, s_tab))
    k_surv = jnp.concatenate([k_surv[:REC], k_surv[PREV:]], axis=0)
    gf_tab = dot_h(f_tab, g)
    rf_one = jnp.broadcast_to(rec[...], (8, 64))
    k_own = jnp.concatenate(
        [
            expand(dot_t(pick_own, s_tab)),
            expand(dot_t(pick_own, f_tab)),
            expand(dot_t(pick_own, gf_tab)),
            expand(dot_t(rf_one, f_tab)),
        ],
        axis=0,
    )

    def indicator(row):
        h = hab[pl.ds(row, SUB), :]
        return jnp.concatenate([jnp.where(h == k, 1.0, 0.0).astype(F32) for k in range(8)], axis=0)

    for kind in range(2):
        for s in range(2):
            rs_all[kind, s] = dot_h(k_surv, indicator(q_row(3 * kind, s)))

    def own_tables(t, carry):
        row = pl.multiple_of(t * SUB, SUB)
        res = dot_h(k_own, indicator(row))
        tabs[t] = res[:384]
        planes[2, pl.ds(pl.multiple_of(HALO + row, SUB), SUB), inner] = res[384:]
        return carry

    lax.fori_loop(0, rows // SUB, own_tables, 0)

    load_s.wait()

    def widen(k, carry):
        st[0, k] = st_raw[0, k].astype(F32)
        st[1, k] = st_raw[1, k].astype(F32)
        return carry

    lax.fori_loop(0, classes, widen, 0)

    for s in range(2):
        far_r[s].wait_recv()
        fwd_r[s].start()
        far_l[s].wait_recv()
        fwd_l[s].start()

    def flat(x):
        return x.reshape(classes * SUB, cols)

    def product(lo, hi):
        a_hi, a_lo = xh[...], xl[...]
        w1, w2 = wh[lo:hi], wl[lo:hi]
        return (
            jnp.dot(w1, a_hi, preferred_element_type=F32)
            + jnp.dot(w1, a_lo, preferred_element_type=F32)
            + jnp.dot(w2, a_hi, preferred_element_type=F32)
        )

    def process(kind, s):
        row = q_row(3 * kind, s)
        prow = pl.multiple_of(HALO + row, SUB)
        blocks = (gath[kind, s, 0], own[:, pl.ds(row, SUB), :], gath[kind, s, 1], gath[kind, s, 2])
        for k, block in enumerate(blocks):
            xh[k * 128 : (k + 1) * 128], xl[k * 128 : (k + 1) * 128] = split(flat(block))
        res = product(0, ROWS_W)
        there = (res[PREV:FAR], res[NEXT:OWN])[kind]
        c1_snd[kind, s] = there.reshape(classes, SUB, cols)
        c1_all[:, pl.ds(row, SUB), :] = res[OWN:REC].reshape(classes, SUB, cols)
        planes[0, pl.ds(prow, SUB), inner] = res[REC : REC + SUB]
        for k, start in enumerate((NEXT, OWN, PREV, FAR)):
            xh[k * 128 : (k + 1) * 128], xl[k * 128 : (k + 1) * 128] = split(
                res[start : start + 128] * rs_all[kind, s, k * 128 : (k + 1) * 128]
            )
        if kind == 0:
            res = product(OWN, FAR)
            mine, seeds, there = res[:128], res[128:136], res[144:272]
        else:
            res = product(NEXT, PREV)
            there, mine, seeds = res[:128], res[128:256], res[256:264]
        d_snd[kind, s] = there.reshape(classes, SUB, cols)
        d_all[:, pl.ds(row, SUB), :] = mine.reshape(classes, SUB, cols)
        planes[1, pl.ds(prow, SUB), inner] = seeds

    def arrive(s):
        near_l[s].wait_recv()
        fwd_l[s].wait_recv()
        near_r[s].wait_recv()
        fwd_r[s].wait_recv()

    arrive(0)
    for kind in range(2):
        process(kind, 0)
        ret_c[kind][0].start()
    arrive(1)
    for kind in range(2):
        process(kind, 1)
    seed_l.start()
    seed_r.start()
    for kind in range(2):
        ret_d[kind][0].start()
    for kind in range(2):
        ret_c[kind][1].start()
    for kind in range(2):
        ret_d[kind][1].start()

    seed_l.wait_recv()
    seed_r.wait_recv()
    halo_d.start()
    halo_u.start()
    halo_d.wait_recv()
    halo_u.wait_recv()
    halo_e.start()
    halo_w.start()
    halo_e.wait_recv()
    halo_w.wait_recv()
    halo_d.wait_send()
    halo_u.wait_send()
    halo_e.wait_send()
    halo_w.wait_send()

    def inside(shape, first):
        y = iota(shape, 0) + (first - HALO) + sy * rows
        x = iota(shape, 1) - SIDE + sx * cols
        return (y >= 0) & (y < nsy * rows) & (x >= 0) & (x < nsx * cols)

    wide = cols + 2 * SIDE
    taps = wr.shape[0]
    reach = taps // 2

    def along_rows(load, row):
        total = wr[0] * load(row - reach)
        for k in range(1, taps):
            total = total + wr[k] * load(row - reach + k)
        return total

    def along_cols(x):
        total = wc[reach] * x
        for k in range(taps):
            if k != reach:
                total = total + wc[k] * pltpu.roll(x, (reach - k) % wide, axis=1)
        return total

    n_pad = rows + 2 * HALO

    for t in range(n_pad // SUB):
        at = pl.ds(t * SUB, SUB)
        mid[at, :] = jnp.where(inside((SUB, wide), t * SUB), planes[0, at, :], 0.0)
    for t in range(1, n_pad // SUB - 1):
        at = pl.ds(t * SUB, SUB)
        spread = along_cols(along_rows(lambda first: mid[pl.ds(first, SUB), :], t * SUB))
        if 2 <= t < 2 + rows // SUB:
            sp1[pl.ds((t - 2) * SUB, SUB), :] = spread[:, SIDE : SIDE + cols]
        seed0[at, :] = jnp.where(
            inside((SUB, wide), t * SUB), planes[1, at, :] + planes[2, at, :] * spread, 0.0
        )
    for t in range(2, 2 + rows // SUB):
        spread = along_cols(along_rows(lambda first: seed0[pl.ds(first, SUB), :], t * SUB))
        sp0[pl.ds((t - 2) * SUB, SUB), :] = spread[:, SIDE : SIDE + cols]

    def finish_c(row):
        at = pl.ds(row, SUB)
        sens_out[1, :, at, :] = st[1, :, at, :] * c1_all[:, at, :]

    def finish_d(row):
        at = pl.ds(row, SUB)
        t = row // SUB
        cube = lambda k: tabs[t, k * 128 : (k + 1) * 128].reshape(classes, SUB, cols)
        carried = d_all[:, at, :] + cube(2) * sp1[at, :][None]
        sens_out[0, :, at, :] = st[0, :, at, :] * carried
        adj_out[:, at, :] = cube(0) * carried + cube(1) * sp0[at, :][None]

    for kind in range(2):
        for s in range(2):
            finish_c(q_row(3 * kind, s))
            finish_d(q_row(3 * kind, s))
    for s in range(2):
        for kind in range(2):
            ret_c[kind][s].wait_recv()
            finish_c(q_row(1 + kind, s))
        for kind in range(2):
            ret_d[kind][s].wait_recv()
            finish_d(q_row(1 + kind, s))
    for group in (far_r, far_l, near_r, near_l, fwd_r, fwd_l, *ret_c, *ret_d, [seed_l, seed_r]):
        for copy in group:
            copy.wait_send()


def per_device(
    adjoint_final, stored_states, habitat, growth, survival, fecundity, recruit, disp_rows, disp_cols
):
    years, classes, rows, cols = stored_states.shape
    wide = cols + 2 * SIDE
    block = (classes, rows, cols)
    vmem = pl.BlockSpec(memory_space=pltpu.VMEM)
    smem = pl.BlockSpec(memory_space=pltpu.SMEM)
    hbm = pl.BlockSpec(memory_space=pl.ANY)
    packs = (2, 2, classes, SUB, cols)
    return pl.pallas_call(
        kernel,
        out_shape=(jax.ShapeDtypeStruct(block, F32), jax.ShapeDtypeStruct((years,) + block, F32)),
        in_specs=[hbm, hbm, vmem, vmem, vmem, vmem, vmem, smem, smem],
        out_specs=(vmem, vmem),
        scratch_shapes=[
            pltpu.VMEM(block, F32),
            pltpu.VMEM((years,) + block, BF16),
            pltpu.VMEM((years,) + block, F32),
            pltpu.VMEM((2, 2, 3, classes, SUB, cols), F32),
            pltpu.VMEM((ROWS_W, 512), BF16),
            pltpu.VMEM((ROWS_W, 512), BF16),
            pltpu.VMEM((512, cols), BF16),
            pltpu.VMEM((512, cols), BF16),
            pltpu.VMEM((2, 2, 512, cols), F32),
            pltpu.VMEM((rows // SUB, 384, cols), F32),
            pltpu.VMEM(block, F32),
            pltpu.VMEM(block, F32),
            pltpu.VMEM(packs, F32),
            pltpu.VMEM(packs, F32),
            pltpu.VMEM((3, rows + 2 * HALO, wide), F32),
            pltpu.VMEM((rows + 2 * HALO, wide), F32),
            pltpu.VMEM((rows + 2 * HALO, wide), F32),
            pltpu.VMEM((rows, cols), F32),
            pltpu.VMEM((rows, cols), F32),
            pltpu.SemaphoreType.DMA((2,)),
            pltpu.SemaphoreType.DMA((26,)),
            pltpu.SemaphoreType.DMA((26,)),
        ],
        compiler_params=pltpu.CompilerParams(
            collective_id=0, has_side_effects=True, vmem_limit_bytes=50 << 20
        ),
        cost_estimate=pl.CostEstimate(flops=4 * 10**9, bytes_accessed=8 * 10**6, transcendentals=0),
    )(
        adjoint_final, stored_states, habitat, growth, survival, fecundity, recruit.reshape(1, -1),
        disp_rows, disp_cols,
    )


def solution(mesh):
    return jax.shard_map(
        per_device,
        mesh=mesh,
        in_specs=(P("cls", "sy", "sx"), P(None, "cls", "sy", "sx"), P("sy", "sx")) + (P(),) * 6,
        out_specs=(P("cls", "sy", "sx"), P(None, "cls", "sy", "sx")),
        check_vma=False,
    )
```

time: 375 us -> 121 us (0.32); the launches traced: 370 us -> 120 us
  waiting for transfers between devices: 248 us -> 0 us
  Pallas kernels: 0 us -> 109 us
  other arithmetic: 50 us -> 0 us
  starting transfers between devices: 25 us -> 0 us
  matrix products: 20.7 us -> 0 us
  between operations: 14 us -> 0.67 us
    reduce_scatter x2 -> x0, waiting for transfers between devices: 158 us -> none  [per_device(): lax.psum_scatter(jnp.einsum('ij,iyx->jyx', growth_rows, current, precisio...]
    pallas_call x0 -> x1, Pallas kernels: none -> 109 us  [per_device(): pl.pallas_call(kernel, out_shape=(jax.ShapeDtypeStruct(block, F32), jax.S...]
    psum x2 -> x0, waiting for transfers between devices: 79.7 us -> none  [per_device(): seed_value = lax.psum(seed_local, 'cls')]
    add x4 -> x0, other arithmetic: 38.5 us -> none  [the longest x2 19.4 us: pass_cols(): result = result + weights[offset] * padded[:, offset:offset + length]]
    ppermute x8 -> x0, starting transfers between devices: 24.8 us -> none  [the longest x4 14.3 us: with_halo(): after = lax.ppermute(leading, axis, down)]
    dot_general x5 -> x0, matrix products: 20.7 us -> none  [the longest x2 14.3 us: per_device(): jnp.einsum('ij,iyx->jyx', growth_rows, current, precision=lax.Precision.H...]
    ppermute x8 -> x0, waiting for transfers between devices: 10.3 us -> none  [the longest x4 9.95 us: with_halo(): after = lax.ppermute(leading, axis, down)]
    another operation x3 -> x0, other arithmetic: 7.84 us -> none  [per_device(): return (adjoint, jnp.stack(sensitivity))]
  transfers between devices with their start and end apart: 12 -> 0, of which waited for: 9 -> 0; matrix products, arithmetic and copies ran while one was open for 17% -> 0% of each run, Pallas kernels for 0% -> 0%
where the time goes in v1:
time: 121 us; the launch traced here: 120 us
  Pallas kernels  109 us (90%)
  local copies, waits for them, and re-layouts  10.5 us (9%)
    pallas_call x1, Pallas kernels, per_device(): pl.pallas_call(kernel, out_shape=(jax.ShapeDtypeStruct(block, F32), jax.S...  109 us
    unnamed x20, local copies, waits for them, and re-layouts  10.5 us

profile of v1, /device:TPU:32, one launch (start us, length us, event | category | flops | bytes accessed | tf_op | source)
XLA Modules:
  0.0 120.3 jit_solution(9300873511581015083)
XLA Ops:
  0.6 0.0 copy-start
  0.6 1.4 %copy-done = f32[16,64,384]{2,1,0:T(8,128)S(1)} copy-done((f32[16,64,384]{2,1,0:T(8,128)S(1)}, f32[16,64,384]{2,1,0:T(8,128)}, u32[]{:S(2)}) %copy-start) | copy-done | bytes 1572888
  2.0 0.0 copy-start.1
  2.0 0.9 copy-done.1
  2.9 0.0 copy-start.2
  2.9 0.8 copy-done.2
  3.7 0.0 copy-start.3
  3.7 0.7 copy-done.3
  4.4 0.0 copy-start.4
  4.4 0.7 copy-done.4
  5.1 0.0 copy-start.5
  5.1 0.7 copy-done.5
  5.7 0.0 copy-start.6
  5.7 0.7 copy-done.6
  6.4 0.0 copy-start.7
  6.4 0.7 copy-done.7
  7.0 109.1 %shard_map.104 = (f32[16,64,384]{2,1,0:T(8,128)S(1)}, f32[2,16,64,384]{3,2,1,0:T(8,128)}) custom-call(f32[16,64,384]{2,1,0:T(8,128)S(1)} %copy-done, bf16[2,16,64,384]{3,2,1,0:T(8,128)(2,1)} %st_hbm.1, s32[64,384]{1,0:T(8,128)S(1)} %copy-done.1, f32[64,64]{1,0:T(8,128)S(1)} %copy-done.2, f32[8,64]{1,0:T(8,128)S(1)} %copy-done.3, f32[8,64]{1,0:T(8,128)S(1)} %copy-done.4, ...), custom_call_target="tpu_custom_call" | custom-call | flops 4000000000 | bytes 8000000 | tf_op jit(solution)/shard_map/pallas_call | solution.py:339
  116.1 0.0 copy-start.8
  116.1 1.1 copy.13
  117.3 1.3 %copy-done.8 = f32[2,16,64,384]{3,2,1,0:T(8,128)S(1)} copy-done((f32[2,16,64,384]{3,2,1,0:T(8,128)S(1)}, f32[2,16,64,384]{3,2,1,0:T(8,128)}, u32[]{:S(2)}) %copy-start.8) | copy-done | bytes 3145752
  118.6 1.7 %copy.14 = f32[2,16,64,384]{3,2,1,0:T(8,128)} copy(f32[2,16,64,384]{3,2,1,0:T(8,128)S(1)} %copy-done.8) | data formatting | bytes 6291456
Async XLA Ops:
  0.6 1.4 %copy-start = (f32[16,64,384]{2,1,0:T(8,128)S(1)}, f32[16,64,384]{2,1,0:T(8,128)}, u32[]{:S(2)}) copy-start(f32[16,64,384]{2,1,0:T(8,128)} %a_hbm.1) | copy-start | bytes 4718596
  2.0 0.9 copy-start.1
  2.9 0.8 copy-start.2
  3.7 0.7 copy-start.3
  4.4 0.7 copy-start.4
  5.1 0.7 copy-start.5
  5.7 0.7 copy-start.6
  6.4 0.7 copy-start.7
  116.1 2.5 %copy-start.8 = (f32[2,16,64,384]{3,2,1,0:T(8,128)S(1)}, f32[2,16,64,384]{3,2,1,0:T(8,128)}, u32[]{:S(2)}) copy-start(f32[2,16,64,384]{3,2,1,0:T(8,128)} %get-tuple-element.5) | copy-start | bytes 9437188

commit v2 on v1

--- a/solution.py
+++ b/solution.py
@@ -37,9 +37,9 @@
 
 
 def kernel(
-    a_hbm, st_hbm, hab, growth, surv, fec, rec, wr, wc,
+    a_hbm, st_hbm, hab_hbm, growth_hbm, surv_hbm, fec_hbm, rec_hbm, wr_hbm, wc_hbm,
     adj_out, sens_out,
-    own, st_raw, st, gath, wh, wl, xh, xl, rs_all, tabs, c1_all, d_all, c1_snd, d_snd, planes, mid, seed0, sp1, sp0,
+    own, st_raw, hab, growth, surv, fec, rec, wr, wc, st, gath, wh, wl, xh, xl, rs_all, tabs, c1_all, d_all, c1_snd, d_snd, planes, mid, seed0, sp1, sp0,
     lsem, send, recv,
 ):
     ncls = 4
@@ -53,14 +53,20 @@
     quarter = rows // ncls
     inner = pl.ds(SIDE, cols)
 
-    load_a = pltpu.make_async_copy(a_hbm, own, lsem.at[0])
-    load_s = pltpu.make_async_copy(st_hbm, st_raw, lsem.at[1])
-    load_a.start()
-    load_s.start()
-
+    loads = [
+        pltpu.make_async_copy(src, dst, lsem.at[k])
+        for k, (src, dst) in enumerate(
+            (
+                (growth_hbm, growth), (surv_hbm, surv), (fec_hbm, fec), (rec_hbm, rec), (hab_hbm, hab),
+                (a_hbm, own), (st_hbm, st_raw), (wr_hbm, wr), (wc_hbm, wc),
+            )
+        )
+    ]
     barrier = pltpu.get_barrier_semaphore()
     for where in ({"cls": left}, {"cls": right}, {"sy": above}, {"sy": below}, {"sx": west}, {"sx": east}):
         pl.semaphore_signal(barrier, inc=1, device_id=where, device_id_type=MESH)
+    for load in loads:
+        load.start()
 
     def q_row(ahead, s):
         return pl.multiple_of(lax.rem(p + ahead, ncls) * quarter + s * SUB, SUB)
@@ -72,16 +78,21 @@
 
     to_right, to_left = {"cls": right}, {"cls": left}
     piece = lambda ref, row: ref.at[:, pl.ds(row, SUB), :]
-    far_r = [remote(piece(own, q_row(1, s)), gath.at[0, s, 1], 0 + s, to_right) for s in range(2)]
-    far_l = [remote(piece(own, q_row(2, s)), gath.at[1, s, 0], 2 + s, to_left) for s in range(2)]
-    near_r = [remote(piece(own, q_row(0, s)), gath.at[1, s, 1], 4 + s, to_right) for s in range(2)]
-    near_l = [remote(piece(own, q_row(3, s)), gath.at[0, s, 0], 6 + s, to_left) for s in range(2)]
+    far_r = [remote(piece(a_hbm, q_row(1, s)), gath.at[0, s, 1], 0 + s, to_right) for s in range(2)]
+    far_l = [remote(piece(a_hbm, q_row(2, s)), gath.at[1, s, 0], 2 + s, to_left) for s in range(2)]
+    near_r = [remote(piece(a_hbm, q_row(0, s)), gath.at[1, s, 1], 4 + s, to_right) for s in range(2)]
+    near_l = [remote(piece(a_hbm, q_row(3, s)), gath.at[0, s, 0], 6 + s, to_left) for s in range(2)]
     fwd_r = [remote(gath.at[0, s, 1], gath.at[1, s, 2], 8 + s, to_right) for s in range(2)]
     fwd_l = [remote(gath.at[1, s, 0], gath.at[0, s, 2], 10 + s, to_left) for s in range(2)]
-    ret_c = [
-        [remote(c1_snd.at[0, s], piece(c1_all, q_row(0, s)), 12 + s, to_left) for s in range(2)],
-        [remote(c1_snd.at[1, s], piece(c1_all, q_row(3, s)), 14 + s, to_right) for s in range(2)],
-    ]
+    half = classes // 2
+
+    def returns(kind, s, k, first):
+        at = pl.ds(first, half)
+        dst = c1_all.at[at, pl.ds(q_row(3 * kind, s), SUB), :]
+        return remote(c1_snd.at[kind, s, at], dst, k, (to_left, to_right)[kind])
+
+    ret_c = [[returns(kind, s, 12 + 2 * kind + s, 0) for s in range(2)] for kind in range(2)]
+    ret_c2 = [[returns(kind, s, 26 + 2 * kind + s, half) for s in range(2)] for kind in range(2)]
     ret_d = [
         [remote(d_snd.at[0, s], piece(d_all, q_row(0, s)), 16 + s, to_left) for s in range(2)],
         [remote(d_snd.at[1, s], piece(d_all, q_row(3, s)), 18 + s, to_right) for s in range(2)],
@@ -104,13 +115,15 @@
     )
 
     pl.semaphore_wait(barrier, 6)
-    load_a.wait()
     for s in range(2):
         far_r[s].start()
         far_l[s].start()
     for s in range(2):
         near_r[s].start()
         near_l[s].start()
+
+    for load in loads:
+        load.wait()
 
     def place_of(rel):
         return ((p + rel) & (ncls - 1)) * classes
@@ -169,8 +182,6 @@
         return carry
 
     lax.fori_loop(0, rows // SUB, own_tables, 0)
-
-    load_s.wait()
 
     def widen(k, carry):
         st[0, k] = st_raw[0, k].astype(F32)
@@ -238,16 +249,19 @@
     seed_l.start()
     seed_r.start()
     for kind in range(2):
-        ret_d[kind][0].start()
-    for kind in range(2):
-        ret_c[kind][1].start()
-    for kind in range(2):
-        ret_d[kind][1].start()
+        ret_c2[kind][0].start()
 
     seed_l.wait_recv()
     seed_r.wait_recv()
     halo_d.start()
     halo_u.start()
+    for kind in range(2):
+        ret_d[kind][0].start()
+    for kind in range(2):
+        ret_c[kind][1].start()
+        ret_c2[kind][1].start()
+    for kind in range(2):
+        ret_d[kind][1].start()
     halo_d.wait_recv()
     halo_u.wait_recv()
     halo_e.start()
@@ -317,11 +331,12 @@
     for s in range(2):
         for kind in range(2):
             ret_c[kind][s].wait_recv()
+            ret_c2[kind][s].wait_recv()
             finish_c(q_row(1 + kind, s))
         for kind in range(2):
             ret_d[kind][s].wait_recv()
             finish_d(q_row(1 + kind, s))
-    for group in (far_r, far_l, near_r, near_l, fwd_r, fwd_l, *ret_c, *ret_d, [seed_l, seed_r]):
+    for group in (far_r, far_l, near_r, near_l, fwd_r, fwd_l, *ret_c, *ret_c2, *ret_d, [seed_l, seed_r]):
         for copy in group:
             copy.wait_send()
 
@@ -333,17 +348,23 @@
     wide = cols + 2 * SIDE
     block = (classes, rows, cols)
     vmem = pl.BlockSpec(memory_space=pltpu.VMEM)
-    smem = pl.BlockSpec(memory_space=pltpu.SMEM)
-    hbm = pl.BlockSpec(memory_space=pl.ANY)
+    hbm = pl.BlockSpec(memory_space=pltpu.HBM)
     packs = (2, 2, classes, SUB, cols)
     return pl.pallas_call(
         kernel,
         out_shape=(jax.ShapeDtypeStruct(block, F32), jax.ShapeDtypeStruct((years,) + block, F32)),
-        in_specs=[hbm, hbm, vmem, vmem, vmem, vmem, vmem, smem, smem],
+        in_specs=[hbm] * 9,
         out_specs=(vmem, vmem),
         scratch_shapes=[
             pltpu.VMEM(block, F32),
             pltpu.VMEM((years,) + block, BF16),
+            pltpu.VMEM(habitat.shape, jnp.int32),
+            pltpu.VMEM(growth.shape, F32),
+            pltpu.VMEM(survival.shape, F32),
+            pltpu.VMEM(fecundity.shape, F32),
+            pltpu.VMEM((1,) + recruit.shape, F32),
+            pltpu.SMEM(disp_rows.shape, F32),
+            pltpu.SMEM(disp_cols.shape, F32),
             pltpu.VMEM((years,) + block, F32),
             pltpu.VMEM((2, 2, 3, classes, SUB, cols), F32),
             pltpu.VMEM((ROWS_W, 512), BF16),
@@ -361,17 +382,22 @@
             pltpu.VMEM((rows + 2 * HALO, wide), F32),
             pltpu.VMEM((rows, cols), F32),
             pltpu.VMEM((rows, cols), F32),
-            pltpu.SemaphoreType.DMA((2,)),
-            pltpu.SemaphoreType.DMA((26,)),
-            pltpu.SemaphoreType.DMA((26,)),
+            pltpu.SemaphoreType.DMA((9,)),
+            pltpu.SemaphoreType.DMA((30,)),
+            pltpu.SemaphoreType.DMA((30,)),
         ],
         compiler_params=pltpu.CompilerParams(
-            collective_id=0, has_side_effects=True, vmem_limit_bytes=50 << 20
+            collective_id=0, has_side_effects=True, vmem_limit_bytes=32 << 20
         ),
         cost_estimate=pl.CostEstimate(flops=4 * 10**9, bytes_accessed=8 * 10**6, transcendentals=0),
     )(
-        adjoint_final, stored_states, habitat, growth, survival, fecundity, recruit.reshape(1, -1),
-        disp_rows, disp_cols,
+        *(
+            pltpu.with_memory_space_constraint(x, pltpu.HBM)
+            for x in (
+                adjoint_final, stored_states, habitat, growth, survival, fecundity, recruit.reshape(1, -1),
+                disp_rows, disp_cols,
+            )
+        )
     )
 
 

time: 121 us -> 102 us (0.84)
  Pallas kernels: 109 us -> 97.4 us
  local copies, waits for them, and re-layouts: 10.5 us -> 2.81 us
    pallas_call x1, Pallas kernels: 109 us -> 97.4 us  [per_device(): pl.pallas_call(kernel, out_shape=(jax.ShapeDtypeStruct(block, F32), jax.S...]
    unnamed x20 -> x2, local copies, waits for them, and re-layouts: 10.5 us -> 2.81 us
where the time goes in v2:
time: 102 us; the launch traced here: 101 us
  Pallas kernels  97.4 us (95%)
  local copies, waits for them, and re-layouts  2.81 us (3%)
    pallas_call x1, Pallas kernels, per_device(): pl.pallas_call(kernel, out_shape=(jax.ShapeDtypeStruct(block, F32), jax.S...  97.4 us
    unnamed x2, local copies, waits for them, and re-layouts  2.81 us

profile of v2, /device:TPU:32, one launch (start us, length us, event | category | flops | bytes accessed | tf_op | source)
XLA Modules:
  0.0 100.8 jit_solution(5819793567983751779)
XLA Ops:
  0.6 97.4 %shard_map.104 = (f32[16,64,384]{2,1,0:T(8,128)S(1)}, f32[2,16,64,384]{3,2,1,0:T(8,128)S(1)}) custom-call(f32[16,64,384]{2,1,0:T(8,128)} %a_hbm.1, bf16[2,16,64,384]{3,2,1,0:T(8,128)(2,1)} %st_hbm.1, s32[64,384]{1,0:T(8,128)} %hab_hbm.1, f32[64,64]{1,0:T(8,128)} %growth_hbm.1, f32[8,64]{1,0:T(8,128)} %surv_hbm.1, f32[8,64]{1,0:T(8,128)} %fec_hbm.1, ...), custom_call_target="tpu_custom_call" | custom-call | flops 4000000000 | bytes 8000000 | tf_op jit(solution)/shard_map/pallas_call | solution.py:353
  98.0 1.1 %copy.13 = f32[16,64,384]{2,1,0:T(8,128)} copy(f32[16,64,384]{2,1,0:T(8,128)S(1)} %get-tuple-element.4) | data formatting | bytes 3145728
  99.2 1.7 %copy.14 = f32[2,16,64,384]{3,2,1,0:T(8,128)} copy(f32[2,16,64,384]{3,2,1,0:T(8,128)S(1)} %get-tuple-element.5) | data formatting | bytes 6291456

commit v3 on v2

--- a/solution.py
+++ b/solution.py
@@ -84,15 +84,10 @@
     near_l = [remote(piece(a_hbm, q_row(3, s)), gath.at[0, s, 0], 6 + s, to_left) for s in range(2)]
     fwd_r = [remote(gath.at[0, s, 1], gath.at[1, s, 2], 8 + s, to_right) for s in range(2)]
     fwd_l = [remote(gath.at[1, s, 0], gath.at[0, s, 2], 10 + s, to_left) for s in range(2)]
-    half = classes // 2
-
-    def returns(kind, s, k, first):
-        at = pl.ds(first, half)
-        dst = c1_all.at[at, pl.ds(q_row(3 * kind, s), SUB), :]
-        return remote(c1_snd.at[kind, s, at], dst, k, (to_left, to_right)[kind])
-
-    ret_c = [[returns(kind, s, 12 + 2 * kind + s, 0) for s in range(2)] for kind in range(2)]
-    ret_c2 = [[returns(kind, s, 26 + 2 * kind + s, half) for s in range(2)] for kind in range(2)]
+    ret_c = [
+        [remote(c1_snd.at[0, s], piece(c1_all, q_row(0, s)), 12 + s, to_left) for s in range(2)],
+        [remote(c1_snd.at[1, s], piece(c1_all, q_row(3, s)), 14 + s, to_right) for s in range(2)],
+    ]
     ret_d = [
         [remote(d_snd.at[0, s], piece(d_all, q_row(0, s)), 16 + s, to_left) for s in range(2)],
         [remote(d_snd.at[1, s], piece(d_all, q_row(3, s)), 18 + s, to_right) for s in range(2)],
@@ -249,17 +244,14 @@
     seed_l.start()
     seed_r.start()
     for kind in range(2):
-        ret_c2[kind][0].start()
+        ret_d[kind][0].start()
 
     seed_l.wait_recv()
     seed_r.wait_recv()
     halo_d.start()
     halo_u.start()
     for kind in range(2):
-        ret_d[kind][0].start()
-    for kind in range(2):
         ret_c[kind][1].start()
-        ret_c2[kind][1].start()
     for kind in range(2):
         ret_d[kind][1].start()
     halo_d.wait_recv()
@@ -331,14 +323,27 @@
     for s in range(2):
         for kind in range(2):
             ret_c[kind][s].wait_recv()
-            ret_c2[kind][s].wait_recv()
             finish_c(q_row(1 + kind, s))
         for kind in range(2):
             ret_d[kind][s].wait_recv()
             finish_d(q_row(1 + kind, s))
-    for group in (far_r, far_l, near_r, near_l, fwd_r, fwd_l, *ret_c, *ret_c2, *ret_d, [seed_l, seed_r]):
+    for group in (far_r, far_l, near_r, near_l, fwd_r, fwd_l, *ret_c, *ret_d, [seed_l, seed_r]):
         for copy in group:
             copy.wait_send()
+
+
+def store(adj_in, sens_in, adj_out, sens_out, sem):
+    classes = adj_in.shape[0]
+    step = classes // 4
+    copies = []
+    for k in range(4):
+        at = pl.ds(k * step, step)
+        for src, dst in ((adj_in, adj_out), (sens_in.at[0], sens_out.at[0]), (sens_in.at[1], sens_out.at[1])):
+            copies.append(pltpu.make_async_copy(src.at[at], dst.at[at], sem.at[len(copies)]))
+    for copy in copies:
+        copy.start()
+    for copy in copies:
+        copy.wait()
 
 
 def per_device(
@@ -350,9 +355,10 @@
     vmem = pl.BlockSpec(memory_space=pltpu.VMEM)
     hbm = pl.BlockSpec(memory_space=pltpu.HBM)
     packs = (2, 2, classes, SUB, cols)
-    return pl.pallas_call(
+    shapes = (jax.ShapeDtypeStruct(block, F32), jax.ShapeDtypeStruct((years,) + block, F32))
+    results = pl.pallas_call(
         kernel,
-        out_shape=(jax.ShapeDtypeStruct(block, F32), jax.ShapeDtypeStruct((years,) + block, F32)),
+        out_shape=shapes,
         in_specs=[hbm] * 9,
         out_specs=(vmem, vmem),
         scratch_shapes=[
@@ -383,8 +389,8 @@
             pltpu.VMEM((rows, cols), F32),
             pltpu.VMEM((rows, cols), F32),
             pltpu.SemaphoreType.DMA((9,)),
-            pltpu.SemaphoreType.DMA((30,)),
-            pltpu.SemaphoreType.DMA((30,)),
+            pltpu.SemaphoreType.DMA((26,)),
+            pltpu.SemaphoreType.DMA((26,)),
         ],
         compiler_params=pltpu.CompilerParams(
             collective_id=0, has_side_effects=True, vmem_limit_bytes=32 << 20
@@ -399,6 +405,14 @@
             )
         )
     )
+    return pl.pallas_call(
+        store,
+        out_shape=shapes,
+        in_specs=[pl.BlockSpec(memory_space=pltpu.VMEM)] * 2,
+        out_specs=(hbm, hbm),
+        scratch_shapes=[pltpu.SemaphoreType.DMA((12,))],
+        compiler_params=pltpu.CompilerParams(vmem_limit_bytes=1 << 20),
+    )(*(pltpu.with_memory_space_constraint(x, pltpu.VMEM) for x in results))
 
 
 def solution(mesh):

time: 102 us -> 102 us (level)
  local copies, waits for them, and re-layouts: 2.81 us -> 0 us
  Pallas kernels: 97.4 us -> 100 us
    unnamed x2 -> x0, local copies, waits for them, and re-layouts: 2.81 us -> none
    pallas_call x1 -> x2, Pallas kernels: 97.4 us -> 100 us  [the longest x1 97.7 us: per_device(): pl.pallas_call(kernel, out_shape=shapes, in_specs=[hbm] * 9, out_specs=(v...]
where the time goes in v3:
time: 102 us; the launch traced here: 101 us
  Pallas kernels  100 us (98%)
    pallas_call x1, Pallas kernels, per_device(): pl.pallas_call(kernel, out_shape=shapes, in_specs=[hbm] * 9, out_specs=(v...  97.7 us
    pallas_call x1, Pallas kernels, per_device(): pl.pallas_call(store, out_shape=shapes, in_specs=[pl.BlockSpec(memory_spa...  2.27 us

profile of v3, /device:TPU:32, one launch (start us, length us, event | category | flops | bytes accessed | tf_op | source)
XLA Modules:
  0.0 100.8 jit_solution(6520035159010206398)
XLA Ops:
  0.6 97.7 %shard_map.104 = (f32[16,64,384]{2,1,0:T(8,128)S(1)}, f32[2,16,64,384]{3,2,1,0:T(8,128)S(1)}) custom-call(f32[16,64,384]{2,1,0:T(8,128)} %a_hbm.1, bf16[2,16,64,384]{3,2,1,0:T(8,128)(2,1)} %st_hbm.1, s32[64,384]{1,0:T(8,128)} %hab_hbm.1, f32[64,64]{1,0:T(8,128)} %growth_hbm.1, f32[8,64]{1,0:T(8,128)} %surv_hbm.1, f32[8,64]{1,0:T(8,128)} %fec_hbm.1, ...), custom_call_target="tpu_custom_call" | custom-call | flops 4000000000 | bytes 8000000 | tf_op jit(solution)/shard_map/pallas_call | solution.py:359
  98.3 2.3 %shard_map.105 = (f32[16,64,384]{2,1,0:T(8,128)}, f32[2,16,64,384]{3,2,1,0:T(8,128)}) custom-call(f32[16,64,384]{2,1,0:T(8,128)S(1)} %get-tuple-element.4.adj_in, f32[2,16,64,384]{3,2,1,0:T(8,128)S(1)} %get-tuple-element.5.sens_in), custom_call_target="tpu_custom_call" | custom-call | tf_op jit(solution)/shard_map/pallas_call | solution.py:408

commit v4 on v3

--- a/solution.py
+++ b/solution.py
@@ -110,12 +110,9 @@
     )
 
     pl.semaphore_wait(barrier, 6)
-    for s in range(2):
-        far_r[s].start()
-        far_l[s].start()
-    for s in range(2):
-        near_r[s].start()
-        near_l[s].start()
+    for first, second in ((far_r[0], far_l[0]), (near_r[0], near_l[0]), (far_r[1], far_l[1])):
+        first.start()
+        second.start()
 
     for load in loads:
         load.wait()
@@ -139,6 +136,13 @@
     wh[...] = w_hi
     wl[...] = w_lo
 
+    far_r[0].wait_recv()
+    fwd_r[0].start()
+    far_l[0].wait_recv()
+    fwd_l[0].start()
+    near_r[1].start()
+    near_l[1].start()
+
     level = jnp.where((iota((64, 8), 0) >> 3) == iota((64, 8), 1), 1.0, 0.0).astype(F32)
 
     def expand(table):
@@ -185,11 +189,10 @@
 
     lax.fori_loop(0, classes, widen, 0)
 
-    for s in range(2):
-        far_r[s].wait_recv()
-        fwd_r[s].start()
-        far_l[s].wait_recv()
-        fwd_l[s].start()
+    far_r[1].wait_recv()
+    fwd_r[1].start()
+    far_l[1].wait_recv()
+    fwd_l[1].start()
 
     def flat(x):
         return x.reshape(classes * SUB, cols)
@@ -251,9 +254,9 @@
     halo_d.start()
     halo_u.start()
     for kind in range(2):
+        ret_d[kind][1].start()
+    for kind in range(2):
         ret_c[kind][1].start()
-    for kind in range(2):
-        ret_d[kind][1].start()
     halo_d.wait_recv()
     halo_u.wait_recv()
     halo_e.start()
@@ -321,12 +324,10 @@
             finish_c(q_row(3 * kind, s))
             finish_d(q_row(3 * kind, s))
     for s in range(2):
-        for kind in range(2):
-            ret_c[kind][s].wait_recv()
-            finish_c(q_row(1 + kind, s))
-        for kind in range(2):
-            ret_d[kind][s].wait_recv()
-            finish_d(q_row(1 + kind, s))
+        for copies, finish in ((ret_c, finish_c), (ret_d, finish_d))[:: 1 - 2 * s]:
+            for kind in range(2):
+                copies[kind][s].wait_recv()
+                finish(q_row(1 + kind, s))
     for group in (far_r, far_l, near_r, near_l, fwd_r, fwd_l, *ret_c, *ret_d, [seed_l, seed_r]):
         for copy in group:
             copy.wait_send()
@@ -334,9 +335,9 @@
 
 def store(adj_in, sens_in, adj_out, sens_out, sem):
     classes = adj_in.shape[0]
-    step = classes // 4
+    step = classes // 1
     copies = []
-    for k in range(4):
+    for k in range(1):
         at = pl.ds(k * step, step)
         for src, dst in ((adj_in, adj_out), (sens_in.at[0], sens_out.at[0]), (sens_in.at[1], sens_out.at[1])):
             copies.append(pltpu.make_async_copy(src.at[at], dst.at[at], sem.at[len(copies)]))
@@ -410,7 +411,7 @@
         out_shape=shapes,
         in_specs=[pl.BlockSpec(memory_space=pltpu.VMEM)] * 2,
         out_specs=(hbm, hbm),
-        scratch_shapes=[pltpu.SemaphoreType.DMA((12,))],
+        scratch_shapes=[pltpu.SemaphoreType.DMA((3,))],
         compiler_params=pltpu.CompilerParams(vmem_limit_bytes=1 << 20),
     )(*(pltpu.with_memory_space_constraint(x, pltpu.VMEM) for x in results))
 

time: 102 us -> 101 us (level)
  no operation moved by 1% of the time
where the time goes in v4:
time: 101 us; the launch traced here: 100 us
  Pallas kernels  99.4 us (98%)
    pallas_call x1, Pallas kernels, per_device(): pl.pallas_call(kernel, out_shape=shapes, in_specs=[hbm] * 9, out_specs=(v...  97.2 us
    pallas_call x1, Pallas kernels, per_device(): pl.pallas_call(store, out_shape=shapes, in_specs=[pl.BlockSpec(memory_spa...  2.21 us

profile of v4, /device:TPU:32, one launch (start us, length us, event | category | flops | bytes accessed | tf_op | source)
XLA Modules:
  0.0 100.2 jit_solution(3206281488339283233)
XLA Ops:
  0.6 97.2 %shard_map.104 = (f32[16,64,384]{2,1,0:T(8,128)S(1)}, f32[2,16,64,384]{3,2,1,0:T(8,128)S(1)}) custom-call(f32[16,64,384]{2,1,0:T(8,128)} %a_hbm.1, bf16[2,16,64,384]{3,2,1,0:T(8,128)(2,1)} %st_hbm.1, s32[64,384]{1,0:T(8,128)} %hab_hbm.1, f32[64,64]{1,0:T(8,128)} %growth_hbm.1, f32[8,64]{1,0:T(8,128)} %surv_hbm.1, f32[8,64]{1,0:T(8,128)} %fec_hbm.1, ...), custom_call_target="tpu_custom_call" | custom-call | flops 4000000000 | bytes 8000000 | tf_op jit(solution)/shard_map/pallas_call | solution.py:360
  97.8 2.2 %shard_map.105 = (f32[16,64,384]{2,1,0:T(8,128)}, f32[2,16,64,384]{3,2,1,0:T(8,128)}) custom-call(f32[16,64,384]{2,1,0:T(8,128)S(1)} %get-tuple-element.4.adj_in, f32[2,16,64,384]{3,2,1,0:T(8,128)S(1)} %get-tuple-element.5.sens_in), custom_call_target="tpu_custom_call" | custom-call | tf_op jit(solution)/shard_map/pallas_call | solution.py:409

commit v5 on v4

--- a/solution.py
+++ b/solution.py
@@ -110,7 +110,7 @@
     )
 
     pl.semaphore_wait(barrier, 6)
-    for first, second in ((far_r[0], far_l[0]), (near_r[0], near_l[0]), (far_r[1], far_l[1])):
+    for first, second in ((far_r[0], far_l[0]), (far_r[1], far_l[1])):
         first.start()
         second.start()
 
@@ -140,8 +140,8 @@
     fwd_r[0].start()
     far_l[0].wait_recv()
     fwd_l[0].start()
-    near_r[1].start()
-    near_l[1].start()
+    near_r[0].start()
+    near_l[0].start()
 
     level = jnp.where((iota((64, 8), 0) >> 3) == iota((64, 8), 1), 1.0, 0.0).astype(F32)
 
@@ -173,6 +173,13 @@
         for s in range(2):
             rs_all[kind, s] = dot_h(k_surv, indicator(q_row(3 * kind, s)))
 
+    far_r[1].wait_recv()
+    fwd_r[1].start()
+    far_l[1].wait_recv()
+    fwd_l[1].start()
+    near_r[1].start()
+    near_l[1].start()
+
     def own_tables(t, carry):
         row = pl.multiple_of(t * SUB, SUB)
         res = dot_h(k_own, indicator(row))
@@ -189,10 +196,6 @@
 
     lax.fori_loop(0, classes, widen, 0)
 
-    far_r[1].wait_recv()
-    fwd_r[1].start()
-    far_l[1].wait_recv()
-    fwd_l[1].start()
 
     def flat(x):
         return x.reshape(classes * SUB, cols)

time: 101 us -> 101 us (level)
  no operation moved by 1% of the time
where the time goes in v5:
time: 101 us; the launch traced here: 100 us
  Pallas kernels  99.4 us (98%)
    pallas_call x1, Pallas kernels, per_device(): pl.pallas_call(kernel, out_shape=shapes, in_specs=[hbm] * 9, out_specs=(v...  97.2 us
    pallas_call x1, Pallas kernels, per_device(): pl.pallas_call(store, out_shape=shapes, in_specs=[pl.BlockSpec(memory_spa...  2.21 us

profile of v5, /device:TPU:32, one launch (start us, length us, event | category | flops | bytes accessed | tf_op | source)
XLA Modules:
  0.0 100.2 jit_solution(2403201970951143489)
XLA Ops:
  0.6 97.2 %shard_map.104 = (f32[16,64,384]{2,1,0:T(8,128)S(1)}, f32[2,16,64,384]{3,2,1,0:T(8,128)S(1)}) custom-call(f32[16,64,384]{2,1,0:T(8,128)} %a_hbm.1, bf16[2,16,64,384]{3,2,1,0:T(8,128)(2,1)} %st_hbm.1, s32[64,384]{1,0:T(8,128)} %hab_hbm.1, f32[64,64]{1,0:T(8,128)} %growth_hbm.1, f32[8,64]{1,0:T(8,128)} %surv_hbm.1, f32[8,64]{1,0:T(8,128)} %fec_hbm.1, ...), custom_call_target="tpu_custom_call" | custom-call | flops 4000000000 | bytes 8000000 | tf_op jit(solution)/shard_map/pallas_call | solution.py:363
  97.8 2.2 %shard_map.105 = (f32[16,64,384]{2,1,0:T(8,128)}, f32[2,16,64,384]{3,2,1,0:T(8,128)}) custom-call(f32[16,64,384]{2,1,0:T(8,128)S(1)} %get-tuple-element.4.adj_in, f32[2,16,64,384]{3,2,1,0:T(8,128)S(1)} %get-tuple-element.5.sens_in), custom_call_target="tpu_custom_call" | custom-call | tf_op jit(solution)/shard_map/pallas_call | solution.py:412

commit v6 on v4

--- a/solution.py
+++ b/solution.py
@@ -98,16 +98,34 @@
 
     seed_l = remote(seed_part(0), seed_part(0), 20, to_left)
     seed_r = remote(seed_part(3), seed_part(3), 21, to_right)
-    halo_d = remote(
-        planes.at[:, pl.ds(rows, HALO), inner], planes.at[:, pl.ds(0, HALO), inner], 22, {"sy": below}
-    )
-    halo_u = remote(
-        planes.at[:, pl.ds(HALO, HALO), inner], planes.at[:, pl.ds(HALO + rows, HALO), inner], 23, {"sy": above}
-    )
-    halo_e = remote(planes.at[:, :, pl.ds(cols, SIDE)], planes.at[:, :, pl.ds(0, SIDE)], 24, {"sx": east})
-    halo_w = remote(
-        planes.at[:, :, pl.ds(SIDE, SIDE)], planes.at[:, :, pl.ds(SIDE + cols, SIDE)], 25, {"sx": west}
-    )
+    def halo_rows(up, k):
+        made = []
+        for n, (which, deep) in enumerate(((pl.ds(0, 1), HALO), (pl.ds(1, 2), SUB))):
+            src = HALO if up else HALO + rows - deep
+            dst = HALO + rows if up else HALO - deep
+            made.append(
+                remote(
+                    planes.at[which, pl.ds(src, deep), inner], planes.at[which, pl.ds(dst, deep), inner],
+                    k + n, {"sy": above if up else below},
+                )
+            )
+        return made
+
+    def halo_cols(back, k):
+        made = []
+        for n, (which, first) in enumerate(((pl.ds(0, 1), 0), (pl.ds(1, 2), SUB))):
+            at = pl.ds(first, rows + 2 * (HALO - first))
+            src, dst = (SIDE, SIDE + cols) if back else (cols, 0)
+            made.append(
+                remote(
+                    planes.at[which, at, pl.ds(src, SIDE)], planes.at[which, at, pl.ds(dst, SIDE)],
+                    k + n, {"sx": west if back else east},
+                )
+            )
+        return made
+
+    row_halos = halo_rows(False, 22) + halo_rows(True, 24)
+    col_halos = halo_cols(False, 26) + halo_cols(True, 28)
 
     pl.semaphore_wait(barrier, 6)
     for first, second in ((far_r[0], far_l[0]), (near_r[0], near_l[0]), (far_r[1], far_l[1])):
@@ -251,22 +269,20 @@
 
     seed_l.wait_recv()
     seed_r.wait_recv()
-    halo_d.start()
-    halo_u.start()
+    for copy in row_halos:
+        copy.start()
     for kind in range(2):
         ret_d[kind][1].start()
     for kind in range(2):
         ret_c[kind][1].start()
-    halo_d.wait_recv()
-    halo_u.wait_recv()
-    halo_e.start()
-    halo_w.start()
-    halo_e.wait_recv()
-    halo_w.wait_recv()
-    halo_d.wait_send()
-    halo_u.wait_send()
-    halo_e.wait_send()
-    halo_w.wait_send()
+    for copy in row_halos:
+        copy.wait_recv()
+    for copy in col_halos:
+        copy.start()
+    for copy in col_halos:
+        copy.wait_recv()
+    for copy in row_halos + col_halos:
+        copy.wait_send()
 
     def inside(shape, first):
         y = iota(shape, 0) + (first - HALO) + sy * rows
@@ -390,8 +406,8 @@
             pltpu.VMEM((rows, cols), F32),
             pltpu.VMEM((rows, cols), F32),
             pltpu.SemaphoreType.DMA((9,)),
-            pltpu.SemaphoreType.DMA((26,)),
-            pltpu.SemaphoreType.DMA((26,)),
+            pltpu.SemaphoreType.DMA((30,)),
+            pltpu.SemaphoreType.DMA((30,)),
         ],
         compiler_params=pltpu.CompilerParams(
             collective_id=0, has_side_effects=True, vmem_limit_bytes=32 << 20

time: 101 us -> 101 us (level)
  no operation moved by 1% of the time
where the time goes in v6:
time: 101 us; the launch traced here: 100 us
  Pallas kernels  99.2 us (98%)
    pallas_call x1, Pallas kernels, per_device(): pl.pallas_call(kernel, out_shape=shapes, in_specs=[hbm] * 9, out_specs=(v...  97 us
    pallas_call x1, Pallas kernels, per_device(): pl.pallas_call(store, out_shape=shapes, in_specs=[pl.BlockSpec(memory_spa...  2.21 us

profile of v6, /device:TPU:32, one launch (start us, length us, event | category | flops | bytes accessed | tf_op | source)
XLA Modules:
  0.0 100.0 jit_solution(4120339727188826100)
XLA Ops:
  0.6 97.0 %shard_map.104 = (f32[16,64,384]{2,1,0:T(8,128)S(1)}, f32[2,16,64,384]{3,2,1,0:T(8,128)S(1)}) custom-call(f32[16,64,384]{2,1,0:T(8,128)} %a_hbm.1, bf16[2,16,64,384]{3,2,1,0:T(8,128)(2,1)} %st_hbm.1, s32[64,384]{1,0:T(8,128)} %hab_hbm.1, f32[64,64]{1,0:T(8,128)} %growth_hbm.1, f32[8,64]{1,0:T(8,128)} %surv_hbm.1, f32[8,64]{1,0:T(8,128)} %fec_hbm.1, ...), custom_call_target="tpu_custom_call" | custom-call | flops 4000000000 | bytes 8000000 | tf_op jit(solution)/shard_map/pallas_call | solution.py:376
  97.7 2.2 %shard_map.105 = (f32[16,64,384]{2,1,0:T(8,128)}, f32[2,16,64,384]{3,2,1,0:T(8,128)}) custom-call(f32[16,64,384]{2,1,0:T(8,128)S(1)} %get-tuple-element.4.adj_in, f32[2,16,64,384]{3,2,1,0:T(8,128)S(1)} %get-tuple-element.5.sens_in), custom_call_target="tpu_custom_call" | custom-call | tf_op jit(solution)/shard_map/pallas_call | solution.py:425
